TPU v7x, 32 devices: a whole 2x2x4 slice. The times are simulated.
32 devices in a mesh: ctx: 8 (over z, core), exp: 4 (over y, x).
Axes of the slice: x: 2, y: 2, z: 4, core: 2. Of those that a mesh axis runs over, the one named last changes fastest.
Arguments:
- x_inner: bfloat16 [2048, 4096], P('ctx', 'exp'), may hold values from -6 to 6
- bc_input: bfloat16 [2048, 256], P('ctx'), may hold values from -6 to 6
- gate_input: bfloat16 [2048, 4096], P('ctx', 'exp'), may hold values from -22 to 22
- conv_weight: float32 [4, 4096], P(None, 'exp'), may hold values from -3 to 3
- bc_conv_weight: float32 [4, 256], replicated, may hold values from -3 to 3
- step_size: float32 [2048, 64], P('ctx', 'exp'), may hold values from 0.002 to 0.05
- log_decay: float32 [2048, 64], P('ctx', 'exp'), may hold values from -1 to 0
- skip_gain: float32 [64], P('exp'), may hold values from 0.5 to 1.5
- norm_gain: float32 [4096], P('exp'), may hold values from 0.25 to 1.75
- out_weight: bfloat16 [4096, 2048], P('exp'), may hold values from -0.09375 to 0.09375
- residual: bfloat16 [2048, 2048], P(('ctx', 'exp')), may hold values from -6 to 6
- moe_gain: float32 [2048], replicated, may hold values from 0.25 to 1.75
- expert_ids: int32 [2048, 4], P(('ctx', 'exp')), may hold values from 0 to 7, all different within a row; in each aligned block of 64 rows (0 to 63, 64 to 127, ...) at most 36 rows name the same one
- route_weights: float32 [2048, 4], P(('ctx', 'exp')), may hold values from 0.1 to 0.6
- gate_up_weight: bfloat16 [8, 2048, 1408], P('exp', 'ctx'), may hold values from -0.125 to 0.125
- down_weight: bfloat16 [8, 704, 2048], P('exp', None, 'ctx'), may hold values from -0.21875 to 0.21875
- out_grad: bfloat16 [2048, 2048], P(('ctx', 'exp')), may hold values from -6 to 6
Outputs:
- layer_output: bfloat16 [2048, 2048], P(('ctx', 'exp'))
- residual_grad: bfloat16 [2048, 2048], P(('ctx', 'exp'))
- route_grads: float32 [2048, 4], P(('ctx', 'exp'))
Inputs may be any that keep to these rules, and one draw needn't show every extreme that they name: `expert_ids`: within the rows of one device (aligned blocks of 64 tokens) no expert is named by more than 36 rows, a bound that some block reaches; each row names 4 different experts.
All inputs are finite; a program needn't handle non-finite values.
Results may differ from a plain program's by a relative error of at most 0.03.
Values may be sent and summed in bfloat16 or wider, within the bound.
A program may use at most 128 MiB of HBM per device.

v0:
```python
import jax
import jax.numpy as jnp
from jax import lax
from jax.sharding import PartitionSpec as P

SPAN = 128
BF = jnp.bfloat16
F32 = jnp.float32


def passed_along(block, axis, distance):
    devices = range(lax.axis_size(axis))
    route = [(i - distance, i) for i in devices if i - distance in devices]
    return lax.ppermute(block, axis, route)


def two_terms(values):
    high = lax.reduce_precision(values, 8, 7)
    return high.astype(BF), (values - high).astype(BF)


def swap(block, axis):
    return lax.all_to_all(block, axis, split_axis=0, concat_axis=0, tiled=True)


def causal_conv(values, weight):
    kernel_len = weight.shape[0]
    row_total = values.shape[0] - kernel_len + 1
    summed = jnp.zeros((row_total, values.shape[1]), F32)
    for offset in range(kernel_len):
        summed = summed + weight[offset][None, :] * values[offset : offset + row_total].astype(F32)
    return summed


def dot(a, b, dims):
    return lax.dot_general(a, b, (dims, ((), ())), preferred_element_type=F32)


def local(
    x_inner,
    bc_input,
    gate_input,
    conv_weight,
    bc_conv_weight,
    step_size,
    log_decay,
    skip_gain,
    norm_gain,
    out_weight,
    residual,
    moe_gain,
    expert_ids,
    route_weights,
    gate_up_weight,
    down_weight,
    out_grad,
):
    ctx, owners = lax.axis_size("ctx"), lax.axis_size("exp")
    local_count = gate_up_weight.shape[0]
    expert_total = local_count * owners
    full_gu, full_down = [], []
    for j in range(local_count):
        full_gu.append(lax.all_gather(gate_up_weight[j], "ctx", axis=0, tiled=True))
        full_down.append(lax.all_gather(down_weight[j], "ctx", axis=1, tiled=True))
    ff_width = down_weight.shape[1]

    tok_rows, model_width = residual.shape
    top_count = expert_ids.shape[1]
    onehot = expert_ids[:, :, None] == jnp.arange(expert_total, dtype=jnp.int32)[None, None, :]
    dense_route = jnp.sum(jnp.where(onehot, route_weights[:, :, None], 0.0), axis=1)
    owned = dense_route.reshape(tok_rows, owners, local_count).transpose(1, 0, 2)
    pad = jnp.zeros((owners, tok_rows, 128 - 2 * local_count), BF)
    grads_sent = jnp.concatenate(
        [
            jnp.broadcast_to(out_grad[None], (owners, tok_rows, model_width)),
            *two_terms(owned),
            pad,
        ],
        axis=2,
    )
    grads_here = swap(grads_sent, "exp").reshape(owners * tok_rows, model_width + 128)
    all_grads = grads_here[:, :model_width]
    route_here = grads_here[:, model_width : model_width + 2 * local_count].astype(F32)
    route_here = route_here[:, :local_count] + route_here[:, local_count:]

    kernel_len = conv_weight.shape[0]
    row_count, channel_count = x_inner.shape
    head_count = step_size.shape[1]
    state_size = bc_input.shape[1] // 2
    head_width = channel_count // head_count
    joined = jnp.concatenate([x_inner, bc_input], axis=1)
    rim_rows = passed_along(joined[row_count - kernel_len + 1 :], "ctx", 1)
    padded = jnp.concatenate([rim_rows, joined], axis=0)
    joint_weight = jnp.concatenate([conv_weight, bc_conv_weight], axis=1)
    convolved = jax.nn.silu(causal_conv(padded, joint_weight)).astype(BF)
    conv_x = convolved[:, :channel_count]
    conv_b = convolved[:, channel_count : channel_count + state_size]
    conv_c = convolved[:, channel_count + state_size :]
    block_count = row_count // SPAN
    x_blocks = conv_x.reshape(block_count, SPAN, head_count, head_width)
    b_blocks = conv_b.reshape(block_count, SPAN, state_size)
    c_blocks = conv_c.reshape(block_count, SPAN, state_size)
    step_blocks = step_size.reshape(block_count, SPAN, head_count)
    decay_blocks = log_decay.reshape(block_count, SPAN, head_count)
    cumulative = jnp.cumsum(decay_blocks, axis=1)

    def wide(per_head):
        shape = per_head.shape
        return jnp.broadcast_to(per_head[..., None], (*shape, head_width)).reshape(
            *shape[:-1], channel_count
        )

    tail_scale = jnp.exp(cumulative[:, -1:, :] - cumulative) * step_blocks
    scaled_x = (
        x_blocks.reshape(block_count, SPAN, channel_count).astype(F32) * wide(tail_scale)
    ).astype(BF)
    states = jnp.einsum("cln,clq->cnq", b_blocks, scaled_x, preferred_element_type=F32)
    block_decay = wide(jnp.exp(cumulative[:, -1, :]))
    held = jnp.zeros((state_size, channel_count), F32)
    factor = jnp.ones((channel_count,), F32)
    local_in, factor_in = [], []
    for j in range(block_count):
        local_in.append(held)
        factor_in.append(factor)
        held = block_decay[j][None, :] * held + states[j]
        factor = factor * block_decay[j]
    part = state_size // ctx
    factor_terms = jnp.concatenate(
        [*(t[None, None, :] for t in two_terms(factor)), jnp.zeros((1, 14, channel_count), BF)],
        axis=1,
    )
    state_sent = jnp.concatenate(
        [
            held.astype(BF).reshape(ctx, part, channel_count),
            jnp.broadcast_to(factor_terms, (ctx, 16, channel_count)),
        ],
        axis=1,
    )
    state_here = swap(state_sent, "ctx").astype(F32)
    running = jnp.zeros((part, channel_count), F32)
    prefixes = []
    for i in range(ctx):
        prefixes.append(running.astype(BF))
        decay_i = state_here[i, part] + state_here[i, part + 1]
        running = decay_i[None, :] * running + state_here[i, :part]
    arriving = swap(jnp.stack(prefixes), "ctx").reshape(state_size, channel_count).astype(F32)

    scores = jnp.einsum("ctn,csn->cts", c_blocks, b_blocks, preferred_element_type=F32)
    causal_mask = (jnp.arange(SPAN)[:, None] >= jnp.arange(SPAN)[None, :])[None, None, :, :]
    cum_h = cumulative.transpose(0, 2, 1)
    step_h = step_blocks.transpose(0, 2, 1)
    gap_matrix = cum_h[:, :, :, None] - cum_h[:, :, None, :]
    weights = jnp.where(
        causal_mask,
        jnp.exp(jnp.where(causal_mask, gap_matrix, 0.0))
        * scores[:, None]
        * step_h[:, :, None, :],
        0.0,
    ).astype(BF)
    within = jnp.einsum("chts,cshp->cthp", weights, x_blocks, preferred_element_type=F32)
    entering = jnp.stack(
        [
            (local_in[j] + factor_in[j][None, :] * arriving).astype(BF)
            for j in range(block_count)
        ]
    )
    carried = jnp.einsum("ctn,cnq->ctq", c_blocks, entering, preferred_element_type=F32) * wide(
        jnp.exp(cumulative)
    )
    mixer_out = (
        within.reshape(row_count, channel_count)
        + carried.reshape(row_count, channel_count)
        + wide(skip_gain)[None, :] * conv_x.astype(F32)
    )
    gated = mixer_out * jax.nn.silu(gate_input.astype(F32))
    squares = jnp.sum(gated * gated, axis=1)
    scaled = (gated * norm_gain[None, :]).astype(BF)
    projected_rows = jnp.dot(scaled, out_weight, preferred_element_type=F32).astype(BF)
    mixed_sent = jnp.concatenate(
        [
            projected_rows,
            *(t[:, None] for t in two_terms(squares)),
            jnp.zeros((row_count, 126), BF),
        ],
        axis=1,
    ).reshape(owners, tok_rows, model_width + 128)
    mixed = jnp.sum(swap(mixed_sent, "exp").astype(F32), axis=0)
    mixed_rows = mixed[:, :model_width]
    own_squares = mixed[:, model_width] + mixed[:, model_width + 1]
    inner_total = channel_count * owners
    hidden_state = (
        residual.astype(F32)
        + mixed_rows * lax.rsqrt(own_squares / inner_total + 1e-05)[:, None]
    ).astype(BF)
    hidden_f = hidden_state.astype(F32)
    inv_rms = lax.rsqrt(jnp.mean(hidden_f * hidden_f, axis=1) + 1e-06)
    normed = (hidden_f * inv_rms[:, None] * moe_gain[None, :]).astype(BF)
    all_normed = swap(
        jnp.broadcast_to(normed[None], (owners, tok_rows, model_width)), "exp"
    ).reshape(owners * tok_rows, model_width)

    out_part = jnp.zeros((owners * tok_rows, model_width), F32)
    grad_part = jnp.zeros((owners * tok_rows, model_width), F32)
    route_part = []
    for j in range(local_count):
        route = route_here[:, j : j + 1]
        projected = dot(all_normed, full_gu[j], ((1,), (0,)))
        pre_gate, pre_up = projected[:, :ff_width], projected[:, ff_width:]
        hidden_grad = dot(all_grads, full_down[j], ((1,), (1,)))
        gate = jax.nn.sigmoid(pre_gate)
        silu_gate = pre_gate * gate
        activated = silu_gate * pre_up
        route_part.append(jnp.sum(activated * hidden_grad, axis=1))
        hidden_grad = hidden_grad * route
        grad_both = jnp.concatenate(
            [
                hidden_grad * pre_up * gate * (1.0 + pre_gate * (1.0 - gate)),
                hidden_grad * silu_gate,
            ],
            axis=1,
        ).astype(BF)
        out_part = out_part + dot((activated * route).astype(BF), full_down[j], ((1,), (0,)))
        grad_part = grad_part + dot(grad_both, full_gu[j], ((1,), (1,)))
    route_terms = two_terms(jnp.stack(route_part, axis=1))
    out_sent = jnp.concatenate(
        [
            out_part.astype(BF),
            *route_terms,
            jnp.zeros((owners * tok_rows, 128 - 2 * local_count), BF),
        ],
        axis=1,
    ).reshape(owners, tok_rows, model_width + 128)
    out_here = swap(out_sent, "exp").astype(F32)
    grad_here = swap(grad_part.astype(BF).reshape(owners, tok_rows, model_width), "exp")
    layer_output = (hidden_f + jnp.sum(out_here[:, :, :model_width], axis=0)).astype(BF)
    route_all = (
        out_here[:, :, model_width : model_width + local_count]
        + out_here[:, :, model_width + local_count : model_width + 2 * local_count]
    )
    route_all = route_all.transpose(1, 0, 2).reshape(tok_rows, 1, expert_total)
    route_grads = jnp.sum(jnp.where(onehot, route_all, 0.0), axis=2)
    normed_grad = jnp.sum(grad_here.astype(F32), axis=0)
    unit_rows = hidden_f * inv_rms[:, None]
    unit_grad = normed_grad * moe_gain[None, :]
    residual_grad = (
        out_grad.astype(F32)
        + inv_rms[:, None]
        * (unit_grad - unit_rows * jnp.mean(unit_grad * unit_rows, axis=1, keepdims=True))
    ).astype(BF)
    return (layer_output, residual_grad, route_grads)


def solution(mesh):
    return jax.shard_map(
        local,
        mesh=mesh,
        in_specs=(
            P("ctx", "exp"),
            P("ctx", None),
            P("ctx", "exp"),
            P(None, "exp"),
            P(),
            P("ctx", "exp"),
            P("ctx", "exp"),
            P("exp"),
            P("exp"),
            P("exp", None),
            P(("ctx", "exp"), None),
            P(),
            P(("ctx", "exp"), None),
            P(("ctx", "exp"), None),
            P("exp", "ctx", None),
            P("exp", None, "ctx"),
            P(("ctx", "exp"), None),
        ),
        out_specs=(P(("ctx", "exp"), None), P(("ctx", "exp"), None), P(("ctx", "exp"), None)),
        check_vma=False,
    )
```

profile of v0, /device:TPU:0, one launch (start us, length us, event | category | flops | bytes accessed | tf_op | source)
XLA Modules:
  0.0 276.3 jit_solution(2914711113976436351)
XLA Ops:
  7.2 2.6 fusion.95
  11.7 2.4 collective-permute-start
  21.5 6.2 %all-to-all-start = ((bf16[8,32,1024]{2,1,0:T(8,128)(2,1)}), bf16[8,32,1024]{2,1,0:T(8,128)(2,1)S(1)}, u32[]{:S(2)}, u32[]{:S(2)}) async-start(bf16[8,32,1024]{2,1,0:T(8,128)(2,1)} %pad_maximum_fusion.1), calls=%async_computation | async-start | bytes 1048576 | tf_op jit(solution)/shard_map/all_to_all | solution.py:23
  33.1 23.7 %all-to-all-done = bf16[8,32,1024]{2,1,0:T(8,128)(2,1)S(1)} async-done(((bf16[8,32,1024]{2,1,0:T(8,128)(2,1)}), bf16[8,32,1024]{2,1,0:T(8,128)(2,1)S(1)}, u32[]{:S(2)}, u32[]{:S(2)}) %all-to-all-start) | async-done | bytes 524320 | tf_op jit(solution)/shard_map/all_to_all | solution.py:23
  61.4 4.3 %all-to-all-start.1 = ((bf16[8,16,1024]{2,1,0:T(8,128)(2,1)}), bf16[8,16,1024]{2,1,0:T(8,128)(2,1)S(1)}, u32[]{:S(2)}, u32[]{:S(2)}) async-start(bf16[8,16,1024]{2,1,0:T(8,128)(2,1)} %fusion.76), calls=%async_computation.1 | async-start | bytes 524288 | tf_op jit(solution)/shard_map/all_to_all | solution.py:23
  65.8 2.2 convolution_bitcast_fusion
  68.1 2.2 copy.220
  70.3 1.6 reshape.522
  71.9 11.1 %all-to-all-done.1 = bf16[8,16,1024]{2,1,0:T(8,128)(2,1)S(1)} async-done(((bf16[8,16,1024]{2,1,0:T(8,128)(2,1)}), bf16[8,16,1024]{2,1,0:T(8,128)(2,1)S(1)}, u32[]{:S(2)}, u32[]{:S(2)}) %all-to-all-start.1) | async-done | bytes 262176 | tf_op jit(solution)/shard_map/all_to_all | solution.py:23
  86.2 3.8 %convolution_convert_fusion = bf16[256,2048]{1,0:T(8,128)(2,1)S(1)} fusion(bf16[1024,2048]{1,0:T(8,128)(2,1)} %param.26, f32[256,1024]{1,0:T(8,128)} %get-tuple-element.15, f32[1024]{0:T(1024)S(1)} %copy-done.29), kind=kOutput, calls=%fused_computation.20 | convolution fusion | flops 1074790400 | bytes 6295552 | tf_op jit(solution)/shard_map/dot_general | solution.py:178
  90.4 1.9 concatenate.41
  92.3 3.6 %all-to-all-start.2 = ((bf16[4,64,2176]{2,1,0:T(8,128)(2,1)}), bf16[4,64,2176]{2,1,0:T(8,128)(2,1)S(1)}, u32[]{:S(2)}, u32[]{:S(2)}) async-start(bf16[4,64,2176]{2,1,0:T(8,128)(2,1)} %concatenate.41), calls=%async_computation.2 | async-start | bytes 2228224 | tf_op jit(solution)/shard_map/all_to_all | solution.py:23
  96.4 1.9 concatenate.42
  98.3 12.5 %all-to-all-done.2 = bf16[4,64,2176]{2,1,0:T(8,128)(2,1)S(1)} async-done(((bf16[4,64,2176]{2,1,0:T(8,128)(2,1)}), bf16[4,64,2176]{2,1,0:T(8,128)(2,1)S(1)}, u32[]{:S(2)}, u32[]{:S(2)}) %all-to-all-start.2) | async-done | bytes 1114144 | tf_op jit(solution)/shard_map/all_to_all | solution.py:23
  110.8 4.3 %all-to-all-start.4 = ((bf16[4,64,2176]{2,1,0:T(8,128)(2,1)}), bf16[4,64,2176]{2,1,0:T(8,128)(2,1)}, u32[]{:S(2)}, u32[]{:S(2)}) async-start(bf16[4,64,2176]{2,1,0:T(8,128)(2,1)} %concatenate.42), calls=%async_computation.4 | async-start | bytes 2228224 | tf_op jit(solution)/shard_map/all_to_all | solution.py:23
  115.8 13.4 %all-to-all-done.4 = bf16[4,64,2176]{2,1,0:T(8,128)(2,1)} async-done(((bf16[4,64,2176]{2,1,0:T(8,128)(2,1)}), bf16[4,64,2176]{2,1,0:T(8,128)(2,1)}, u32[]{:S(2)}, u32[]{:S(2)}) %all-to-all-start.4) | async-done | bytes 1114144 | tf_op jit(solution)/shard_map/all_to_all | solution.py:23
  130.3 3.7 %all-to-all-start.3 = ((bf16[4,64,2048]{2,1,0:T(8,128)(2,1)}), bf16[4,64,2048]{2,1,0:T(8,128)(2,1)S(1)}, u32[]{:S(2)}, u32[]{:S(2)}) async-start(bf16[4,64,2048]{2,1,0:T(8,128)(2,1)} %broadcast_in_dim.156), calls=%async_computation.3 | async-start | bytes 2097152 | tf_op jit(solution)/shard_map/all_to_all | solution.py:23
  135.2 11.7 %all-to-all-done.3 = bf16[4,64,2048]{2,1,0:T(8,128)(2,1)S(1)} async-done(((bf16[4,64,2048]{2,1,0:T(8,128)(2,1)}), bf16[4,64,2048]{2,1,0:T(8,128)(2,1)S(1)}, u32[]{:S(2)}, u32[]{:S(2)}) %all-to-all-start.3) | async-done | bytes 1048608 | tf_op jit(solution)/shard_map/all_to_all | solution.py:23
  146.9 5.6 %fusion.2 = f32[256,1408]{1,0:T(8,128)} fusion(bf16[256,2048]{1,0:T(8,128)(2,1)S(1)} %bitcast.110, bf16[1,2048,1408]{2,1,0:T(8,128)(2,1)} %all-gather.13.cloned.1.call-done), kind=kOutput, calls=%fused_computation.2 | convolution fusion | flops 1476395008 | bytes 8257536 | tf_op jit(solution)/shard_map/dot_general | solution.py:36
  152.5 4.0 %multiply_convert_fusion.3 = (bf16[256,704]{1,0:T(8,128)(2,1)S(1)}, bf16[256,704]{1,0:T(8,128)(2,1)S(1)}, f32[256]{0:T(256)S(1)}) fusion(f32[256,1408]{1,0:T(8,128)} %fusion.2, f32[256]{0:T(256)S(1)} %get-tuple-element.7, bf16[1,704,2048]{2,1,0:T(8,128)(2,1)} %all-gather.15.cloned.1.call-done, bf16[256,2176]{1,0:T(8,128)(2,1)} %bitcast.30), kind=kOutput, calls=%fused_computation.52 | convolution fusion | flops 741261056 | bytes 6227968 | tf_op jit(solution)/shard_map/dot_general | solution.py:36
  156.9 3.3 %fusion = f32[256,2048]{1,0:T(8,128)} fusion(bf16[1,2048,1408]{2,1,0:T(8,128)(2,1)S(1)} %copy-done.26, bf16[256,704]{1,0:T(8,128)(2,1)S(1)} %get-tuple-element.25, bf16[256,704]{1,0:T(8,128)(2,1)S(1)} %get-tuple-element.24), kind=kOutput, calls=%fused_computation | convolution fusion | flops 1477836800 | bytes 8585216 | tf_op jit(solution)/shard_map/dot_general | solution.py:36
  160.2 27.2 %all-gather.9.cloned.1.call-done = bf16[1,2048,1408]{2,1,0:T(8,128)(2,1)} async-done(((bf16[1,256,1408]{2,1,0:T(8,128)(2,1)}), bf16[1,2048,1408]{2,1,0:T(8,128)(2,1)}) %all-gather.9.cloned.1.call-update) | async-done | bytes 5767184 | tf_op jit(solution)/shard_map/all_gather | solution.py:63
  187.3 5.5 %fusion.6 = f32[256,1408]{1,0:T(8,128)} fusion(bf16[256,2048]{1,0:T(8,128)(2,1)S(1)} %bitcast.111, bf16[1,2048,1408]{2,1,0:T(8,128)(2,1)} %all-gather.9.cloned.1.call-done), kind=kOutput, calls=%fused_computation.6 | convolution fusion | flops 1476395008 | bytes 8257536 | tf_op jit(solution)/shard_map/dot_general | solution.py:36
  192.9 31.7 %all-gather.11.cloned.1.call-done = bf16[1,704,2048]{2,1,0:T(8,128)(2,1)} async-done(((bf16[1,704,256]{2,1,0:T(8,128)(2,1)}), bf16[1,704,2048]{2,1,0:T(8,128)(2,1)}) %all-gather.11.cloned.1.call-update) | async-done | bytes 2883600 | tf_op jit(solution)/shard_map/all_gather | solution.py:64
  224.5 4.0 %multiply_convert_fusion.5 = (bf16[256,704]{1,0:T(8,128)(2,1)S(1)}, bf16[256,704]{1,0:T(8,128)(2,1)S(1)}, f32[256]{0:T(256)S(1)}) fusion(f32[256,1408]{1,0:T(8,128)} %fusion.6, f32[256]{0:T(256)S(1)} %get-tuple-element.6, bf16[1,704,2048]{2,1,0:T(8,128)(2,1)} %all-gather.11.cloned.1.call-done, bf16[256,2176]{1,0:T(8,128)(2,1)} %bitcast.30), kind=kOutput, calls=%fused_computation.54 | convolution fusion | flops 741261056 | bytes 6227968 | tf_op jit(solution)/shard_map/dot_general | solution.py:36
  229.5 2.9 %fusion.22 = bf16[256,2048]{1,0:T(8,128)(2,1)} fusion(f32[256,2048]{1,0:T(8,128)S(1)} %copy-done.30, bf16[1,2048,1408]{2,1,0:T(8,128)(2,1)S(1)} %copy-done.27, bf16[256,704]{1,0:T(8,128)(2,1)S(1)} %get-tuple-element.23, bf16[256,704]{1,0:T(8,128)(2,1)S(1)} %get-tuple-element.22), kind=kOutput, calls=%fused_computation.18 | convolution fusion | flops 1478885376 | bytes 9633792 | tf_op jit(solution)/shard_map/dot_general | solution.py:36
  232.3 3.7 %all-to-all-start.6 = ((bf16[4,64,2048]{2,1,0:T(8,128)(2,1)}), bf16[4,64,2048]{2,1,0:T(8,128)(2,1)S(1)}, u32[]{:S(2)}, u32[]{:S(2)}) async-start(bf16[4,64,2048]{2,1,0:T(8,128)(2,1)} %bitcast.37), calls=%async_computation.6 | async-start | bytes 2097152 | tf_op jit(solution)/shard_map/all_to_all | solution.py:23
  236.3 3.5 %fusion.10 = f32[256,2048]{1,0:T(8,128)S(1)} fusion(bf16[1,704,2048]{2,1,0:T(8,128)(2,1)} %all-gather.15.cloned.1.call-done, f32[256]{0:T(256)S(1)} %get-tuple-element.7, f32[256,1408]{1,0:T(8,128)} %fusion.2), kind=kOutput, calls=%fused_computation.10 | convolution fusion | flops 739459072 | bytes 6554624 | tf_op jit(solution)/shard_map/dot_general | solution.py:36
  241.0 1.9 concatenate.43
  243.0 7.2 %all-to-all-done.6 = bf16[4,64,2048]{2,1,0:T(8,128)(2,1)S(1)} async-done(((bf16[4,64,2048]{2,1,0:T(8,128)(2,1)}), bf16[4,64,2048]{2,1,0:T(8,128)(2,1)S(1)}, u32[]{:S(2)}, u32[]{:S(2)}) %all-to-all-start.6) | async-done | bytes 1048608 | tf_op jit(solution)/shard_map/all_to_all | solution.py:23
  250.2 3.5 %all-to-all-start.5 = ((bf16[4,64,2176]{2,1,0:T(8,128)(2,1)}), bf16[4,64,2176]{2,1,0:T(8,128)(2,1)S(1)}, u32[]{:S(2)}, u32[]{:S(2)}) async-start(bf16[4,64,2176]{2,1,0:T(8,128)(2,1)} %bitcast.36), calls=%async_computation.5 | async-start | bytes 2228224 | tf_op jit(solution)/shard_map/all_to_all | solution.py:23
  254.1 13.6 %all-to-all-done.5 = bf16[4,64,2176]{2,1,0:T(8,128)(2,1)S(1)} async-done(((bf16[4,64,2176]{2,1,0:T(8,128)(2,1)}), bf16[4,64,2176]{2,1,0:T(8,128)(2,1)S(1)}, u32[]{:S(2)}, u32[]{:S(2)}) %all-to-all-start.5) | async-done | bytes 1114144 | tf_op jit(solution)/shard_map/all_to_all | solution.py:23
  (168 shorter events, 31.4 us)
Async XLA Ops:
  7.2 139.7 %all-gather.13.cloned.1.call-start = ((), (), s32[]{:S(2)}) async-start(), calls=%async_computation.9 | async-start | bytes 6488064 | tf_op jit(solution)/shard_map/all_gather | solution.py:63
  9.9 4.3 %copy-start.16 = (f32[256,16]{0,1:T(8,128)S(1)}, f32[256,16]{0,1:T(8,128)}, u32[]{:S(2)}) copy-start(f32[256,16]{0,1:T(8,128)} %param.22) | copy-start | bytes 49156
  9.9 4.4 %copy-start.17 = (f32[256,16]{0,1:T(8,128)S(1)}, f32[256,16]{0,1:T(8,128)}, u32[]{:S(2)}) copy-start(f32[256,16]{0,1:T(8,128)} %param.23) | copy-start | bytes 49156
  9.9 5.1 %copy-start.20 = (f32[4,1024]{1,0:T(4,128)S(1)}, f32[4,1024]{1,0:T(4,128)}, u32[]{:S(2)}) copy-start(f32[4,1024]{1,0:T(4,128)} %param.20) | copy-start | bytes 49156
  9.9 5.0 %copy-start.23 = (f32[4,256]{1,0:T(4,128)S(1)}, f32[4,256]{1,0:T(4,128)}, u32[]{:S(2)}) copy-start(f32[4,256]{1,0:T(4,128)} %param.21) | copy-start | bytes 12292
  9.9 142.6 %all-gather.15.cloned.1.call-start = ((), (), s32[]{:S(2)}) async-start(), calls=%async_computation.10 | async-start | bytes 3244032 | tf_op jit(solution)/shard_map/all_gather | solution.py:64
  10.9 176.4 %all-gather.9.cloned.1.call-start = ((), (), s32[]{:S(2)}) async-start(), calls=%async_computation.7 | async-start | bytes 6488064 | tf_op jit(solution)/shard_map/all_gather | solution.py:63
  11.7 6.1 %collective-permute-start = (bf16[3,1280]{1,0:T(4,128)(2,1)S(1)}, bf16[3,1280]{1,0:T(4,128)(2,1)S(1)}, u32[]{:S(2)}, u32[]{:S(2)}) collective-permute-start(bf16[3,1280]{1,0:T(4,128)(2,1)S(1)} %slice.246), channel_id=1, source_target_pairs={{0,4},{4,8},{8,12},{12,16},{16,20},{20,24},{24,28},{1,5},{5,9},{9,... | collective-permute-start | bytes 23048 | tf_op jit(solution)/shard_map/ppermute | solution.py:14
  20.0 8.3 %copy-start.25 = (f32[16]{0:T(128)S(1)}, f32[16]{0:T(128)}, u32[]{:S(2)}) copy-start(f32[16]{0:T(128)} %param.24) | copy-start | bytes 196
  20.2 9.6 %copy-start.6 = (f32[2,128,16]{2,1,0:T(8,128)S(1)}, f32[2,128,16]{2,1,0:T(8,128)}, u32[]{:S(2)}) copy-start(f32[2,128,16]{2,1,0:T(8,128)} %get-tuple-element.48) | copy-start | bytes 49156
  21.5 35.3 %all-to-all-start = ((bf16[8,32,1024]{2,1,0:T(8,128)(2,1)}), bf16[8,32,1024]{2,1,0:T(8,128)(2,1)S(1)}, u32[]{:S(2)}, u32[]{:S(2)}) async-start(bf16[8,32,1024]{2,1,0:T(8,128)(2,1)} %pad_maximum_fusion.1), calls=%async_computation | async-start | bytes 1048576 | tf_op jit(solution)/shard_map/all_to_all | solution.py:23
  27.6 196.9 %all-gather.11.cloned.1.call-start = ((), (), s32[]{:S(2)}) async-start(), calls=%async_computation.8 | async-start | bytes 3244032 | tf_op jit(solution)/shard_map/all_gather | solution.py:64
  33.1 32.7 %copy-start.18 = (f32[2,16,128]{2,1,0:T(8,128)S(1)}, f32[2,16,128]{2,1,0:T(8,128)}, u32[]{:S(2)}) copy-start(f32[2,16,128]{2,1,0:T(8,128)} %copy.189) | copy-start | bytes 49156
  33.1 32.7 %copy-start.19 = (f32[2,16,128]{2,1,0:T(8,128)S(1)}, f32[2,16,128]{2,1,0:T(8,128)}, u32[]{:S(2)}) copy-start(f32[2,16,128]{2,1,0:T(8,128)} %copy.186) | copy-start | bytes 49156
  33.1 32.7 %copy-start.21 = (pred[128,128]{1,0:T(8,128)(4,1)S(1)}, pred[128,128]{1,0:T(8,128)(4,1)}, u32[]{:S(2)}) copy-start(pred[128,128]{1,0:T(8,128)(4,1)} %iota_compare_fusion) | copy-start | bytes 49156
  61.4 21.5 %all-to-all-start.1 = ((bf16[8,16,1024]{2,1,0:T(8,128)(2,1)}), bf16[8,16,1024]{2,1,0:T(8,128)(2,1)S(1)}, u32[]{:S(2)}, u32[]{:S(2)}) async-start(bf16[8,16,1024]{2,1,0:T(8,128)(2,1)} %fusion.76), calls=%async_computation.1 | async-start | bytes 524288 | tf_op jit(solution)/shard_map/all_to_all | solution.py:23
  70.3 12.7 %copy-start.14 = (f32[1024]{0:T(1024)S(1)}, f32[1024]{0:T(1024)}, u32[]{:S(2)}) copy-start(f32[1024]{0:T(1024)} %copy-done.13) | copy-start | bytes 12292
  71.9 12.7 %copy-start.1 = (bf16[256,1280]{1,0:T(8,128)(2,1)S(1)}, bf16[256,1280]{1,0:T(8,128)(2,1)}, u32[]{:S(2)}) copy-start(bf16[256,1280]{1,0:T(8,128)(2,1)} %copy-done) | copy-start | bytes 1966084
  71.9 12.7 %copy-start.2 = (f32[256,1024]{1,0:T(8,128)S(1)}, f32[256,1024]{1,0:T(8,128)}, u32[]{:S(2)}) copy-start(f32[256,1024]{1,0:T(8,128)} %reshape.522) | copy-start | bytes 3145732
  90.3 5.6 %copy-start.22 = (s32[64,4]{0,1:T(4,128)S(1)}, s32[64,4]{0,1:T(4,128)}, u32[]{:S(2)}) copy-start(s32[64,4]{0,1:T(4,128)} %param.29) | copy-start | bytes 3076
  90.3 5.6 %copy-start.24 = (f32[64,4]{0,1:T(4,128)S(1)}, f32[64,4]{0,1:T(4,128)}, u32[]{:S(2)}) copy-start(f32[64,4]{0,1:T(4,128)} %param.30) | copy-start | bytes 3076
  90.4 5.9 %copy-start.3 = (bf16[64,2048]{1,0:T(8,128)(2,1)S(1)}, bf16[64,2048]{1,0:T(8,128)(2,1)}, u32[]{:S(2)}) copy-start(bf16[64,2048]{1,0:T(8,128)(2,1)} %param.33) | copy-start | bytes 786436
  92.3 18.5 %all-to-all-start.2 = ((bf16[4,64,2176]{2,1,0:T(8,128)(2,1)}), bf16[4,64,2176]{2,1,0:T(8,128)(2,1)S(1)}, u32[]{:S(2)}, u32[]{:S(2)}) async-start(bf16[4,64,2176]{2,1,0:T(8,128)(2,1)} %concatenate.41), calls=%async_computation.2 | async-start | bytes 2228224 | tf_op jit(solution)/shard_map/all_to_all | solution.py:23
  98.3 17.1 %copy-start.8 = (bf16[64,2048]{1,0:T(8,128)(2,1)S(1)}, bf16[64,2048]{1,0:T(8,128)(2,1)}, u32[]{:S(2)}) copy-start(bf16[64,2048]{1,0:T(8,128)(2,1)} %param.27) | copy-start | bytes 786436
  98.3 17.4 %copy-start.11 = (f32[2048]{0:T(1024)S(1)}, f32[2048]{0:T(1024)}, u32[]{:S(2)}) copy-start(f32[2048]{0:T(1024)} %param.28) | copy-start | bytes 24580
  110.8 18.4 %all-to-all-start.4 = ((bf16[4,64,2176]{2,1,0:T(8,128)(2,1)}), bf16[4,64,2176]{2,1,0:T(8,128)(2,1)}, u32[]{:S(2)}, u32[]{:S(2)}) async-start(bf16[4,64,2176]{2,1,0:T(8,128)(2,1)} %concatenate.42), calls=%async_computation.4 | async-start | bytes 2228224 | tf_op jit(solution)/shard_map/all_to_all | solution.py:23
  130.3 16.6 %all-to-all-start.3 = ((bf16[4,64,2048]{2,1,0:T(8,128)(2,1)}), bf16[4,64,2048]{2,1,0:T(8,128)(2,1)S(1)}, u32[]{:S(2)}, u32[]{:S(2)}) async-start(bf16[4,64,2048]{2,1,0:T(8,128)(2,1)} %broadcast_in_dim.156), calls=%async_computation.3 | async-start | bytes 2097152 | tf_op jit(solution)/shard_map/all_to_all | solution.py:23
  152.5 4.4 %copy-start.26 = (bf16[1,2048,1408]{2,1,0:T(8,128)(2,1)S(1)}, bf16[1,2048,1408]{2,1,0:T(8,128)(2,1)}, u32[]{:S(2)}) copy-start(bf16[1,2048,1408]{2,1,0:T(8,128)(2,1)} %all-gather.13.cloned.1.call-done) | copy-start | bytes 17301508
  224.5 4.3 %copy-start.27 = (bf16[1,2048,1408]{2,1,0:T(8,128)(2,1)S(1)}, bf16[1,2048,1408]{2,1,0:T(8,128)(2,1)}, u32[]{:S(2)}) copy-start(bf16[1,2048,1408]{2,1,0:T(8,128)(2,1)} %all-gather.9.cloned.1.call-done) | copy-start | bytes 17301508
  224.5 4.9 %copy-start.30 = (f32[256,2048]{1,0:T(8,128)S(1)}, f32[256,2048]{1,0:T(8,128)}, u32[]{:S(2)}) copy-start(f32[256,2048]{1,0:T(8,128)} %fusion) | copy-start | bytes 6291460
  232.3 17.8 %all-to-all-start.6 = ((bf16[4,64,2048]{2,1,0:T(8,128)(2,1)}), bf16[4,64,2048]{2,1,0:T(8,128)(2,1)S(1)}, u32[]{:S(2)}, u32[]{:S(2)}) async-start(bf16[4,64,2048]{2,1,0:T(8,128)(2,1)} %bitcast.37), calls=%async_computation.6 | async-start | bytes 2097152 | tf_op jit(solution)/shard_map/all_to_all | solution.py:23
  250.2 17.5 %all-to-all-start.5 = ((bf16[4,64,2176]{2,1,0:T(8,128)(2,1)}), bf16[4,64,2176]{2,1,0:T(8,128)(2,1)S(1)}, u32[]{:S(2)}, u32[]{:S(2)}) async-start(bf16[4,64,2176]{2,1,0:T(8,128)(2,1)} %bitcast.36), calls=%async_computation.5 | async-start | bytes 2228224 | tf_op jit(solution)/shard_map/all_to_all | solution.py:23
  (12 other events, 21.3 us)
Sparse Core Ops, SparseCore 0:
  10.0 79.7 all-gather.12
  91.4 35.5 all-gather.14
  128.6 58.6 all-gather.8
  188.8 35.7 all-gather.10
where the time goes:
time: 277 us; the launch traced here: 276 us
  waiting for transfers between devices  153 us (55%)
  matrix products  38.1 us (14%)
  starting transfers between devices  31.8 us (11%)
  local copies, waits for them, and re-layouts  23.9 us (9%)
  other arithmetic  15 us (5%)
  between operations  14.4 us (5%)
    all_to_all x7, waiting for transfers between devices, swap(): return lax.all_to_all(block, axis, split_axis=0, concat_axis=0, tiled=True)  93 us
    all_gather x2, waiting for transfers between devices, local(): full_down.append(lax.all_gather(down_weight[j], 'ctx', axis=1, tiled=True))  31.7 us
    dot_general x8, matrix products, dot(): return lax.dot_general(a, b, (dims, ((), ())), preferred_element_type=F32)  30 us
    all_to_all x7, starting transfers between devices, swap(): return lax.all_to_all(block, axis, split_axis=0, concat_axis=0, tiled=True)  29.3 us
    all_gather x2, waiting for transfers between devices, local(): full_gu.append(lax.all_gather(gate_up_weight[j], 'ctx', axis=0, tiled=True))  27.2 us
  transfers between devices with their start and end apart: 12, of which 9 were waited for; matrix products, arithmetic and copies ran while one was open for 23% of the time, Pallas kernels for 0%

commit v1 on v0

--- a/solution.py
+++ b/solution.py
@@ -1,6 +1,10 @@
+import functools
+
 import jax
 import jax.numpy as jnp
 from jax import lax
+from jax.experimental import pallas as pl
+from jax.experimental.pallas import tpu as pltpu
 from jax.sharding import PartitionSpec as P
 
 SPAN = 128
@@ -34,6 +38,102 @@
 
 def dot(a, b, dims):
     return lax.dot_general(a, b, (dims, ((), ())), preferred_element_type=F32)
+
+
+def chip_ring(chips):
+    return [0, *range(1, chips, 2), *[c for c in range(chips - 1, 0, -1) if c % 2 == 0]]
+
+
+def gathered(shard, order):
+    chips = len(order)
+    along = [
+        (2 * order[t] + core, 2 * order[(t + 1) % chips] + core)
+        for t in range(chips)
+        for core in range(2)
+    ]
+    across = [(i, i ^ 1) for i in range(2 * chips)]
+    held, slots = shard, []
+    for step in range(chips):
+        later = lax.ppermute(held, "ctx", along) if step < chips - 1 else None
+        slots += [held, lax.ppermute(held, "ctx", across)]
+        held = later
+    return slots
+
+
+def experts_kernel(count, width, places, x_ref, g_ref, route_ref, *refs):
+    gus, downs = refs[:count], refs[count : 2 * count]
+    out_ref, grad_ref, pair_ref, out_acc, grad_acc = refs[2 * count :]
+    depth = gus[0].shape[1]
+    columns = [pl.ds(pl.multiple_of(places[k] * depth, depth), depth) for k in range(count)]
+    pair_ref[...] = jnp.zeros_like(pair_ref)
+    for j in range(gus[0].shape[0]):
+        projected = dot(x_ref[:, columns[0]], gus[0][j], ((1,), (0,)))
+        hidden_grad = dot(g_ref[:, columns[0]], downs[0][j], ((1,), (1,)))
+        for k in range(1, count):
+            projected += dot(x_ref[:, columns[k]], gus[k][j], ((1,), (0,)))
+            hidden_grad += dot(g_ref[:, columns[k]], downs[k][j], ((1,), (1,)))
+        route = route_ref[:, j : j + 1]
+        pre_gate, pre_up = projected[:, :width], projected[:, width:]
+        gate = jax.nn.sigmoid(pre_gate)
+        silu_gate = pre_gate * gate
+        activated = silu_gate * pre_up
+        pair_ref[:, j : j + 1] = jnp.sum(activated * hidden_grad, axis=1, keepdims=True)
+        hidden_grad = hidden_grad * route
+        grad_both = jnp.concatenate(
+            [
+                hidden_grad * pre_up * gate * (1.0 + pre_gate * (1.0 - gate)),
+                hidden_grad * silu_gate,
+            ],
+            axis=1,
+        ).astype(BF)
+        activated = (activated * route).astype(BF)
+        for k in range(count):
+            out_k = dot(activated, downs[k][j], ((1,), (0,)))
+            grad_k = dot(grad_both, gus[k][j], ((1,), (1,)))
+            if j > 0:
+                out_k += out_acc[:, columns[k]]
+                grad_k += grad_acc[:, columns[k]]
+            if j < gus[0].shape[0] - 1:
+                out_acc[:, columns[k]] = out_k
+                grad_acc[:, columns[k]] = grad_k
+            else:
+                out_ref[:, columns[k]] = out_k.astype(BF)
+                grad_ref[:, columns[k]] = grad_k.astype(BF)
+
+
+def experts(places, x, g, route, gus, downs):
+    rows, model_width = x.shape
+    tile, count, width = 256, len(gus), downs[0].shape[1]
+
+    def whole(a):
+        return pl.BlockSpec(a.shape, lambda i: (0, 0, 0), pipeline_mode=pl.Buffered(1))
+
+    wide_rows = pl.BlockSpec((tile, model_width), lambda i: (i, 0))
+    lane_rows = pl.BlockSpec((tile, 128), lambda i: (i, 0))
+    flops = 12 * rows * model_width * width * gus[0].shape[0]
+    return pl.pallas_call(
+        functools.partial(experts_kernel, count, width),
+        grid=(rows // tile,),
+        in_specs=[
+            pl.BlockSpec(memory_space=pltpu.SMEM),
+            wide_rows,
+            wide_rows,
+            lane_rows,
+            *[whole(a) for a in gus],
+            *[whole(a) for a in downs],
+        ],
+        out_specs=[wide_rows, wide_rows, lane_rows],
+        out_shape=[
+            jax.ShapeDtypeStruct((rows, model_width), BF),
+            jax.ShapeDtypeStruct((rows, model_width), BF),
+            jax.ShapeDtypeStruct((rows, 128), F32),
+        ],
+        scratch_shapes=[pltpu.VMEM((tile, model_width), F32)] * 2,
+        compiler_params=pltpu.CompilerParams(vmem_limit_bytes=56 * 2**20),
+        cost_estimate=pl.CostEstimate(
+            flops=flops, bytes_accessed=24 * 2**20, transcendentals=rows * width
+        ),
+    )(places, x, g, route, *gus, *downs)
 
 
 def local(
@@ -58,31 +158,22 @@
     ctx, owners = lax.axis_size("ctx"), lax.axis_size("exp")
     local_count = gate_up_weight.shape[0]
     expert_total = local_count * owners
-    full_gu, full_down = [], []
-    for j in range(local_count):
-        full_gu.append(lax.all_gather(gate_up_weight[j], "ctx", axis=0, tiled=True))
-        full_down.append(lax.all_gather(down_weight[j], "ctx", axis=1, tiled=True))
-    ff_width = down_weight.shape[1]
+    order = chip_ring(ctx // 2)
+    place = lax.axis_index("ctx")
+    chip, core = place // 2, place % 2
+    ring_place = jnp.array([order.index(c) for c in range(ctx // 2)], jnp.int32)[chip]
+    sources = jnp.array(order, jnp.int32)[
+        (ring_place - jnp.arange(ctx // 2, dtype=jnp.int32)) % (ctx // 2)
+    ]
+    places = jnp.stack([2 * sources + core, 2 * sources + 1 - core], axis=1).reshape(ctx)
+    gus = gathered(gate_up_weight, order)
+    downs = gathered(down_weight, order)
 
     tok_rows, model_width = residual.shape
     top_count = expert_ids.shape[1]
     onehot = expert_ids[:, :, None] == jnp.arange(expert_total, dtype=jnp.int32)[None, None, :]
     dense_route = jnp.sum(jnp.where(onehot, route_weights[:, :, None], 0.0), axis=1)
     owned = dense_route.reshape(tok_rows, owners, local_count).transpose(1, 0, 2)
-    pad = jnp.zeros((owners, tok_rows, 128 - 2 * local_count), BF)
-    grads_sent = jnp.concatenate(
-        [
-            jnp.broadcast_to(out_grad[None], (owners, tok_rows, model_width)),
-            *two_terms(owned),
-            pad,
-        ],
-        axis=2,
-    )
-    grads_here = swap(grads_sent, "exp").reshape(owners * tok_rows, model_width + 128)
-    all_grads = grads_here[:, :model_width]
-    route_here = grads_here[:, model_width : model_width + 2 * local_count].astype(F32)
-    route_here = route_here[:, :local_count] + route_here[:, local_count:]
-
     kernel_len = conv_weight.shape[0]
     row_count, channel_count = x_inner.shape
     head_count = step_size.shape[1]
@@ -184,7 +275,24 @@
         ],
         axis=1,
     ).reshape(owners, tok_rows, model_width + 128)
-    mixed = jnp.sum(swap(mixed_sent, "exp").astype(F32), axis=0)
+    mixed_back = swap(mixed_sent, "exp")
+    pad = jnp.zeros((owners, tok_rows, 128 - 2 * local_count), BF)
+    out_grad_late, mixed_back = lax.optimization_barrier((out_grad, mixed_back))
+    grads_sent = jnp.concatenate(
+        [
+            jnp.broadcast_to(out_grad_late[None], (owners, tok_rows, model_width)),
+            *two_terms(owned),
+            pad,
+        ],
+        axis=2,
+    )
+    grads_here = swap(grads_sent, "exp").reshape(owners * tok_rows, model_width + 128)
+    all_grads = grads_here[:, :model_width]
+    route_here = grads_here[:, model_width : model_width + 2 * local_count].astype(F32)
+    route_here = route_here[:, :local_count] + route_here[:, local_count:]
+    route_here = jnp.pad(route_here, ((0, 0), (0, 128 - local_count)))
+
+    mixed = jnp.sum(mixed_back.astype(F32), axis=0)
     mixed_rows = mixed[:, :model_width]
     own_squares = mixed[:, model_width] + mixed[:, model_width + 1]
     inner_total = channel_count * owners
@@ -199,39 +307,20 @@
         jnp.broadcast_to(normed[None], (owners, tok_rows, model_width)), "exp"
     ).reshape(owners * tok_rows, model_width)
 
-    out_part = jnp.zeros((owners * tok_rows, model_width), F32)
-    grad_part = jnp.zeros((owners * tok_rows, model_width), F32)
-    route_part = []
-    for j in range(local_count):
-        route = route_here[:, j : j + 1]
-        projected = dot(all_normed, full_gu[j], ((1,), (0,)))
-        pre_gate, pre_up = projected[:, :ff_width], projected[:, ff_width:]
-        hidden_grad = dot(all_grads, full_down[j], ((1,), (1,)))
-        gate = jax.nn.sigmoid(pre_gate)
-        silu_gate = pre_gate * gate
-        activated = silu_gate * pre_up
-        route_part.append(jnp.sum(activated * hidden_grad, axis=1))
-        hidden_grad = hidden_grad * route
-        grad_both = jnp.concatenate(
-            [
-                hidden_grad * pre_up * gate * (1.0 + pre_gate * (1.0 - gate)),
-                hidden_grad * silu_gate,
-            ],
-            axis=1,
-        ).astype(BF)
-        out_part = out_part + dot((activated * route).astype(BF), full_down[j], ((1,), (0,)))
-        grad_part = grad_part + dot(grad_both, full_gu[j], ((1,), (1,)))
-    route_terms = two_terms(jnp.stack(route_part, axis=1))
+    out_part, grad_part, route_part = experts(
+        places, all_normed, all_grads, route_here, gus, downs
+    )
+    route_terms = two_terms(route_part[:, :local_count])
     out_sent = jnp.concatenate(
         [
-            out_part.astype(BF),
+            out_part,
             *route_terms,
             jnp.zeros((owners * tok_rows, 128 - 2 * local_count), BF),
         ],
         axis=1,
     ).reshape(owners, tok_rows, model_width + 128)
     out_here = swap(out_sent, "exp").astype(F32)
-    grad_here = swap(grad_part.astype(BF).reshape(owners, tok_rows, model_width), "exp")
+    grad_here = swap(grad_part.reshape(owners, tok_rows, model_width), "exp")
     layer_output = (hidden_f + jnp.sum(out_here[:, :, :model_width], axis=0)).astype(BF)
     route_all = (
         out_here[:, :, model_width : model_width + local_count]

time: 277 us -> 260 us (0.939)
  matrix products: 38.1 us -> 6.46 us
  Pallas kernels: 0 us -> 18.6 us
  between operations: 14.4 us -> 1.29 us
  starting transfers between devices: 31.8 us -> 39.9 us
    ppermute x0 -> x14, waiting for transfers between devices: none -> 95.9 us  [the longest x6 95.8 us: gathered(): later = lax.ppermute(held, 'ctx', along) if step < chips - 1 else None]
    all_gather x4 -> x0, waiting for transfers between devices: 58.8 us -> none  [the longest x2 31.7 us: local(): full_down.append(lax.all_gather(down_weight[j], 'ctx', axis=1, tiled=True))]
    all_to_all x7, waiting for transfers between devices: 93 us -> 57.6 us  [swap(): return lax.all_to_all(block, axis, split_axis=0, concat_axis=0, tiled=True)]
    dot_general x8 -> x0, matrix products: 30 us -> none  [dot(): return lax.dot_general(a, b, (dims, ((), ())), preferred_element_type=F32)]
    pallas_call x0 -> x1, Pallas kernels: none -> 18.6 us  [experts(): pl.pallas_call(functools.partial(experts_kernel, count, width), grid=(row...]
    ppermute x0 -> x14, starting transfers between devices: none -> 7.87 us  [the longest x6 6.21 us: gathered(): later = lax.ppermute(held, 'ctx', along) if step < chips - 1 else None]
  transfers between devices with their start and end apart: 12 -> 22, of which waited for: 9 -> 10; matrix products, arithmetic and copies ran while one was open for 23% -> 13% of each run, Pallas kernels for 0% -> 0%
where the time goes in v1:
time: 260 us; the launch traced here: 259 us
  waiting for transfers between devices  153 us (59%)
  starting transfers between devices  39.9 us (15%)
  local copies, waits for them, and re-layouts  26.3 us (10%)
  Pallas kernels  18.6 us (7%)
  other arithmetic  12.9 us (5%)
  matrix products  6.46 us (2%)
    ppermute x6, waiting for transfers between devices, gathered(): later = lax.ppermute(held, 'ctx', along) if step < chips - 1 else None  95.8 us
    all_to_all x7, waiting for transfers between devices, swap(): return lax.all_to_all(block, axis, split_axis=0, concat_axis=0, tiled=True)  57.6 us
    all_to_all x7, starting transfers between devices, swap(): return lax.all_to_all(block, axis, split_axis=0, concat_axis=0, tiled=True)  29.7 us
    pallas_call x1, Pallas kernels, experts(): pl.pallas_call(functools.partial(experts_kernel, count, width), grid=(row...  18.6 us
    ppermute x6, starting transfers between devices, gathered(): later = lax.ppermute(held, 'ctx', along) if step < chips - 1 else None  6.21 us
  transfers between devices with their start and end apart: 22, of which 10 were waited for; matrix products, arithmetic and copies ran while one was open for 13% of the time, Pallas kernels for 0%

profile of v1, /device:TPU:0, one launch (start us, length us, event | category | flops | bytes accessed | tf_op | source)
XLA Modules:
  0.0 259.0 jit_solution(1598585200094965898)
XLA Ops:
  2.7 2.4 collective-permute-start
  10.1 7.7 %all-to-all-start = ((bf16[8,32,1024]{2,1,0:T(8,128)(2,1)}), bf16[8,32,1024]{2,1,0:T(8,128)(2,1)S(1)}, u32[]{:S(2)}, u32[]{:S(2)}) async-start(bf16[8,32,1024]{2,1,0:T(8,128)(2,1)} %pad_maximum_fusion.1), calls=%async_computation | async-start | bytes 1048576 | tf_op jit(solution)/shard_map/all_to_all | solution.py:27
  17.7 2.0 collective-permute-start.2
  19.7 2.4 collective-permute-start.9
  22.3 1.3 copy.146
  27.0 6.5 %all-to-all-done = bf16[8,32,1024]{2,1,0:T(8,128)(2,1)S(1)} async-done(((bf16[8,32,1024]{2,1,0:T(8,128)(2,1)}), bf16[8,32,1024]{2,1,0:T(8,128)(2,1)S(1)}, u32[]{:S(2)}, u32[]{:S(2)}) %all-to-all-start) | async-done | bytes 524320 | tf_op jit(solution)/shard_map/all_to_all | solution.py:27
  38.2 3.4 %all-to-all-start.1 = ((bf16[8,16,1024]{2,1,0:T(8,128)(2,1)}), bf16[8,16,1024]{2,1,0:T(8,128)(2,1)S(1)}, u32[]{:S(2)}, u32[]{:S(2)}) async-start(bf16[8,16,1024]{2,1,0:T(8,128)(2,1)} %fusion.37), calls=%async_computation.1 | async-start | bytes 524288 | tf_op jit(solution)/shard_map/all_to_all | solution.py:27
  41.8 22.9 %collective-permute-done.2.refs_2_ = bf16[2,256,1408]{2,1,0:T(8,128)(2,1)} collective-permute-done((bf16[2,256,1408]{2,1,0:T(8,128)(2,1)}, bf16[2,256,1408]{2,1,0:T(8,128)(2,1)}, u32[]{:S(2)}, u32[]{:S(2)}) %collective-permute-start.2) | collective-permute-done | bytes 1441824 | tf_op jit(solution)/shard_map/ppermute | solution.py:57
  64.7 2.2 convolution_bitcast_fusion
  66.9 2.2 copy.162
  69.1 1.5 reshape.607
  70.6 15.0 %all-to-all-done.1 = bf16[8,16,1024]{2,1,0:T(8,128)(2,1)S(1)} async-done(((bf16[8,16,1024]{2,1,0:T(8,128)(2,1)}), bf16[8,16,1024]{2,1,0:T(8,128)(2,1)S(1)}, u32[]{:S(2)}, u32[]{:S(2)}) %all-to-all-start.1) | async-done | bytes 262176 | tf_op jit(solution)/shard_map/all_to_all | solution.py:27
  87.9 3.4 %convolution_convert_fusion = bf16[256,2048]{1,0:T(8,128)(2,1)S(1)} fusion(bf16[1024,2048]{1,0:T(8,128)(2,1)} %param.28, f32[256,1024]{1,0:T(8,128)S(1)} %get-tuple-element.23, f32[1024]{0:T(1024)S(1)} %copy-done.25), kind=kOutput, calls=%fused_computation.1 | convolution fusion | flops 1074790400 | bytes 6295552 | tf_op jit(solution)/shard_map/dot_general | solution.py:269
  91.4 24.7 %collective-permute-done.4.refs_4_ = bf16[2,256,1408]{2,1,0:T(8,128)(2,1)} collective-permute-done((bf16[2,256,1408]{2,1,0:T(8,128)(2,1)}, bf16[2,256,1408]{2,1,0:T(8,128)(2,1)}, u32[]{:S(2)}, u32[]{:S(2)}) %collective-permute-start.4) | collective-permute-done | bytes 1441824 | tf_op jit(solution)/shard_map/ppermute | solution.py:57
  116.4 2.0 concatenate.33
  118.4 3.9 %all-to-all-start.2 = ((bf16[4,64,2176]{2,1,0:T(8,128)(2,1)}), bf16[4,64,2176]{2,1,0:T(8,128)(2,1)S(1)}, u32[]{:S(2)}, u32[]{:S(2)}) async-start(bf16[4,64,2176]{2,1,0:T(8,128)(2,1)} %concatenate.33), calls=%async_computation.2 | async-start | bytes 2228224 | tf_op jit(solution)/shard_map/all_to_all | solution.py:27
  122.2 1.8 collective-permute-start.11
  126.2 1.1 gather_fusion
  127.3 38.6 %collective-permute-done.11.refs_12_ = bf16[2,704,256]{2,1,0:T(8,128)(2,1)} collective-permute-done((bf16[2,704,256]{2,1,0:T(8,128)(2,1)}, bf16[2,704,256]{2,1,0:T(8,128)(2,1)}, u32[]{:S(2)}, u32[]{:S(2)}) %collective-permute-start.11) | collective-permute-done | bytes 720928 | tf_op jit(solution)/shard_map/ppermute | solution.py:57
  166.0 1.9 concatenate.34
  168.0 3.7 %all-to-all-start.4 = ((bf16[4,64,2176]{2,1,0:T(8,128)(2,1)}), bf16[4,64,2176]{2,1,0:T(8,128)(2,1)S(1)}, u32[]{:S(2)}, u32[]{:S(2)}) async-start(bf16[4,64,2176]{2,1,0:T(8,128)(2,1)} %concatenate.34), calls=%async_computation.4 | async-start | bytes 2228224 | tf_op jit(solution)/shard_map/all_to_all | solution.py:27
  174.2 9.6 %collective-permute-done.13.refs_14_ = bf16[2,704,256]{2,1,0:T(8,128)(2,1)} collective-permute-done((bf16[2,704,256]{2,1,0:T(8,128)(2,1)}, bf16[2,704,256]{2,1,0:T(8,128)(2,1)}, u32[]{:S(2)}, u32[]{:S(2)}) %collective-permute-start.13) | collective-permute-done | bytes 720928 | tf_op jit(solution)/shard_map/ppermute | solution.py:57
  183.9 1.1 all-to-all-done.4
  185.0 1.1 broadcast_in_dim.157
  186.1 3.8 %all-to-all-start.3 = ((bf16[4,64,2048]{2,1,0:T(8,128)(2,1)}), bf16[4,64,2048]{2,1,0:T(8,128)(2,1)S(1)}, u32[]{:S(2)}, u32[]{:S(2)}) async-start(bf16[4,64,2048]{2,1,0:T(8,128)(2,1)} %broadcast_in_dim.157), calls=%async_computation.3 | async-start | bytes 2097152 | tf_op jit(solution)/shard_map/all_to_all | solution.py:27
  192.6 10.6 %all-to-all-done.3 = bf16[4,64,2048]{2,1,0:T(8,128)(2,1)S(1)} async-done(((bf16[4,64,2048]{2,1,0:T(8,128)(2,1)}), bf16[4,64,2048]{2,1,0:T(8,128)(2,1)S(1)}, u32[]{:S(2)}, u32[]{:S(2)}) %all-to-all-start.3) | async-done | bytes 1048608 | tf_op jit(solution)/shard_map/all_to_all | solution.py:27
  204.3 18.6 %shard_map.202 = (bf16[256,2048]{1,0:T(8,128)(2,1)}, bf16[256,2048]{1,0:T(8,128)(2,1)}, f32[256,128]{1,0:T(8,128)}) custom-call(s32[8]{0:T(128)} %reshape.591.places, bf16[256,2048]{1,0:T(8,128)(2,1)} %bitcast.83, bf16[256,2048]{1,0:T(8,128)(2,1)} %slice.252.g_ref, f32[256,128]{1,0:T(8,128)} %pad.4.route_ref, bf16[2,256,1408]{2,1,0:T(8,128)(2,1)} %refs_0_.1, ...), custom_call_target="tpu_custom_call" | custom-call | flops 8858370048 | bytes 25165824 | tf_op jit(solution)/shard_map/pallas_call | solution.py:114
  222.9 3.7 %all-to-all-start.6 = ((bf16[4,64,2048]{2,1,0:T(8,128)(2,1)}), bf16[4,64,2048]{2,1,0:T(8,128)(2,1)S(1)}, u32[]{:S(2)}, u32[]{:S(2)}) async-start(bf16[4,64,2048]{2,1,0:T(8,128)(2,1)} %bitcast.84), calls=%async_computation.6 | async-start | bytes 2097152 | tf_op jit(solution)/shard_map/all_to_all | solution.py:27
  226.6 1.9 concatenate.35
  228.6 11.0 %all-to-all-done.6 = bf16[4,64,2048]{2,1,0:T(8,128)(2,1)S(1)} async-done(((bf16[4,64,2048]{2,1,0:T(8,128)(2,1)}), bf16[4,64,2048]{2,1,0:T(8,128)(2,1)S(1)}, u32[]{:S(2)}, u32[]{:S(2)}) %all-to-all-start.6) | async-done | bytes 1048608 | tf_op jit(solution)/shard_map/all_to_all | solution.py:27
  239.6 3.5 %all-to-all-start.5 = ((bf16[4,64,2176]{2,1,0:T(8,128)(2,1)}), bf16[4,64,2176]{2,1,0:T(8,128)(2,1)S(1)}, u32[]{:S(2)}, u32[]{:S(2)}) async-start(bf16[4,64,2176]{2,1,0:T(8,128)(2,1)} %bitcast.34), calls=%async_computation.5 | async-start | bytes 2228224 | tf_op jit(solution)/shard_map/all_to_all | solution.py:27
  243.5 13.3 %all-to-all-done.5 = bf16[4,64,2176]{2,1,0:T(8,128)(2,1)S(1)} async-done(((bf16[4,64,2176]{2,1,0:T(8,128)(2,1)}), bf16[4,64,2176]{2,1,0:T(8,128)(2,1)S(1)}, u32[]{:S(2)}, u32[]{:S(2)}) %all-to-all-start.5) | async-done | bytes 1114144 | tf_op jit(solution)/shard_map/all_to_all | solution.py:27
  (170 shorter events, 28.6 us)
Async XLA Ops:
  0.7 5.2 %copy-start.20 = (f32[4,256]{1,0:T(4,128)S(1)}, f32[4,256]{1,0:T(4,128)}, u32[]{:S(2)}) copy-start(f32[4,256]{1,0:T(4,128)} %param.23) | copy-start | bytes 12292
  2.7 3.7 %collective-permute-start = (bf16[3,1280]{1,0:T(4,128)(2,1)S(1)}, bf16[3,1280]{1,0:T(4,128)(2,1)S(1)}, u32[]{:S(2)}, u32[]{:S(2)}) collective-permute-start(bf16[3,1280]{1,0:T(4,128)(2,1)S(1)} %slice.212), channel_id=1, source_target_pairs={{0,4},{4,8},{8,12},{12,16},{16,20},{20,24},{24,28},{1,5},{5,9},{9,... | collective-permute-start | bytes 23048 | tf_op jit(solution)/shard_map/ppermute | solution.py:18
  10.1 23.5 %all-to-all-start = ((bf16[8,32,1024]{2,1,0:T(8,128)(2,1)}), bf16[8,32,1024]{2,1,0:T(8,128)(2,1)S(1)}, u32[]{:S(2)}, u32[]{:S(2)}) async-start(bf16[8,32,1024]{2,1,0:T(8,128)(2,1)} %pad_maximum_fusion.1), calls=%async_computation | async-start | bytes 1048576 | tf_op jit(solution)/shard_map/all_to_all | solution.py:27
  17.7 46.9 %collective-permute-start.2 = (bf16[2,256,1408]{2,1,0:T(8,128)(2,1)}, bf16[2,256,1408]{2,1,0:T(8,128)(2,1)}, u32[]{:S(2)}, u32[]{:S(2)}) collective-permute-start(bf16[2,256,1408]{2,1,0:T(8,128)(2,1)} %refs_0_.1), channel_id=1, source_target_pairs={{0,8},{4,12},{8,24},{12,28},{24,16},{28,20},{16,0},{20,4},{1,9},{5... | collective-permute-start | bytes 4325384 | tf_op jit(solution)/shard_map/ppermute | solution.py:57
  19.7 102.5 %collective-permute-start.9 = (bf16[2,704,256]{2,1,0:T(8,128)(2,1)}, bf16[2,704,256]{2,1,0:T(8,128)(2,1)}, u32[]{:S(2)}, u32[]{:S(2)}) collective-permute-start(bf16[2,704,256]{2,1,0:T(8,128)(2,1)} %refs_8_.1), channel_id=1, source_target_pairs={{0,8},{4,12},{8,24},{12,28},{24,16},{28,20},{16,0},{20,4},{1,9},{5... | collective-permute-start | bytes 2162696 | tf_op jit(solution)/shard_map/ppermute | solution.py:57
  33.7 31.0 %copy-start.15 = (f32[2,16,128]{2,1,0:T(8,128)S(1)}, f32[2,16,128]{2,1,0:T(8,128)}, u32[]{:S(2)}) copy-start(f32[2,16,128]{2,1,0:T(8,128)} %copy.135) | copy-start | bytes 49156
  33.7 31.0 %copy-start.16 = (f32[2,16,128]{2,1,0:T(8,128)S(1)}, f32[2,16,128]{2,1,0:T(8,128)}, u32[]{:S(2)}) copy-start(f32[2,16,128]{2,1,0:T(8,128)} %copy.138) | copy-start | bytes 49156
  33.7 31.0 %copy-start.18 = (pred[128,128]{1,0:T(8,128)(4,1)S(1)}, pred[128,128]{1,0:T(8,128)(4,1)}, u32[]{:S(2)}) copy-start(pred[128,128]{1,0:T(8,128)(4,1)} %iota_compare_fusion) | copy-start | bytes 49156
  38.2 47.4 %all-to-all-start.1 = ((bf16[8,16,1024]{2,1,0:T(8,128)(2,1)}), bf16[8,16,1024]{2,1,0:T(8,128)(2,1)S(1)}, u32[]{:S(2)}, u32[]{:S(2)}) async-start(bf16[8,16,1024]{2,1,0:T(8,128)(2,1)} %fusion.37), calls=%async_computation.1 | async-start | bytes 524288 | tf_op jit(solution)/shard_map/all_to_all | solution.py:27
  64.7 51.4 %collective-permute-start.4 = (bf16[2,256,1408]{2,1,0:T(8,128)(2,1)}, bf16[2,256,1408]{2,1,0:T(8,128)(2,1)}, u32[]{:S(2)}, u32[]{:S(2)}) collective-permute-start(bf16[2,256,1408]{2,1,0:T(8,128)(2,1)} %collective-permute-done.2.refs_2_), channel_id=1, source_target_pairs={{0,8},{4,12},{8,24},{12,28},{24,16},{28,20},{16,0},{20,4},{1,9},{5... | collective-permute-start | bytes 4325384 | tf_op jit(solution)/shard_map/ppermute | solution.py:57
  70.6 15.1 %copy-start.4 = (f32[2,128,1024]{2,1,0:T(8,128)S(1)}, f32[2,128,1024]{2,1,0:T(8,128)}, u32[]{:S(2)}) copy-start(f32[2,128,1024]{2,1,0:T(8,128)} %copy.146) | copy-start | bytes 3145732
  116.1 57.4 %collective-permute-start.6 = (bf16[2,256,1408]{2,1,0:T(8,128)(2,1)}, bf16[2,256,1408]{2,1,0:T(8,128)(2,1)}, u32[]{:S(2)}, u32[]{:S(2)}) collective-permute-start(bf16[2,256,1408]{2,1,0:T(8,128)(2,1)} %collective-permute-done.4.refs_4_), channel_id=1, source_target_pairs={{0,8},{4,12},{8,24},{12,28},{24,16},{28,20},{16,0},{20,4},{1,9},{5... | collective-permute-start | bytes 4325384 | tf_op jit(solution)/shard_map/ppermute | solution.py:57
  118.4 6.2 %copy-start.19 = (s32[64,4]{0,1:T(4,128)S(1)}, s32[64,4]{0,1:T(4,128)}, u32[]{:S(2)}) copy-start(s32[64,4]{0,1:T(4,128)} %param.31) | copy-start | bytes 3076
  118.4 6.2 %copy-start.21 = (f32[64,4]{0,1:T(4,128)S(1)}, f32[64,4]{0,1:T(4,128)}, u32[]{:S(2)}) copy-start(f32[64,4]{0,1:T(4,128)} %param.32) | copy-start | bytes 3076
  118.4 6.5 %copy-start = (s32[4]{0:T(128)S(1)}, s32[4]{0:T(128)}, u32[]{:S(2)}) copy-start(s32[4]{0:T(128)} %constant.82.clone) | copy-start | bytes 52
  118.4 47.5 %copy-start.8 = (bf16[64,2048]{1,0:T(8,128)(2,1)S(1)}, bf16[64,2048]{1,0:T(8,128)(2,1)}, u32[]{:S(2)}) copy-start(bf16[64,2048]{1,0:T(8,128)(2,1)} %param.35) | copy-start | bytes 786436
  118.4 47.5 %all-to-all-start.2 = ((bf16[4,64,2176]{2,1,0:T(8,128)(2,1)}), bf16[4,64,2176]{2,1,0:T(8,128)(2,1)S(1)}, u32[]{:S(2)}, u32[]{:S(2)}) async-start(bf16[4,64,2176]{2,1,0:T(8,128)(2,1)} %concatenate.33), calls=%async_computation.2 | async-start | bytes 2228224 | tf_op jit(solution)/shard_map/all_to_all | solution.py:27
  122.2 43.6 %collective-permute-start.11 = (bf16[2,704,256]{2,1,0:T(8,128)(2,1)}, bf16[2,704,256]{2,1,0:T(8,128)(2,1)}, u32[]{:S(2)}, u32[]{:S(2)}) collective-permute-start(bf16[2,704,256]{2,1,0:T(8,128)(2,1)} %collective-permute-done.9.refs_10_), channel_id=1, source_target_pairs={{0,8},{4,12},{8,24},{12,28},{24,16},{28,20},{16,0},{20,4},{1,9},{5... | collective-permute-start | bytes 2162696 | tf_op jit(solution)/shard_map/ppermute | solution.py:57
  124.1 49.7 %collective-permute-start.1 = (bf16[2,256,1408]{2,1,0:T(8,128)(2,1)}, bf16[2,256,1408]{2,1,0:T(8,128)(2,1)}, u32[]{:S(2)}, u32[]{:S(2)}) collective-permute-start(bf16[2,256,1408]{2,1,0:T(8,128)(2,1)} %refs_0_.1), channel_id=1, source_target_pairs={{0,4},{4,0},{8,12},{12,8},{16,20},{20,16},{24,28},{28,24},{1,5},{5... | collective-permute-start | bytes 4325384 | tf_op jit(solution)/shard_map/ppermute | solution.py:58
  124.1 48.9 %collective-permute-start.8 = (bf16[2,704,256]{2,1,0:T(8,128)(2,1)}, bf16[2,704,256]{2,1,0:T(8,128)(2,1)S(1)}, u32[]{:S(2)}, u32[]{:S(2)}) collective-permute-start(bf16[2,704,256]{2,1,0:T(8,128)(2,1)} %refs_8_.1), channel_id=1, source_target_pairs={{0,4},{4,0},{8,12},{12,8},{16,20},{20,16},{24,28},{28,24},{1,5},{5... | collective-permute-start | bytes 2162696 | tf_op jit(solution)/shard_map/ppermute | solution.py:58
  125.5 47.5 %collective-permute-start.10 = (bf16[2,704,256]{2,1,0:T(8,128)(2,1)}, bf16[2,704,256]{2,1,0:T(8,128)(2,1)}, u32[]{:S(2)}, u32[]{:S(2)}) collective-permute-start(bf16[2,704,256]{2,1,0:T(8,128)(2,1)} %collective-permute-done.9.refs_10_), channel_id=1, source_target_pairs={{0,4},{4,0},{8,12},{12,8},{16,20},{20,16},{24,28},{28,24},{1,5},{5... | collective-permute-start | bytes 2162696 | tf_op jit(solution)/shard_map/ppermute | solution.py:58
  165.9 18.0 %collective-permute-start.13 = (bf16[2,704,256]{2,1,0:T(8,128)(2,1)}, bf16[2,704,256]{2,1,0:T(8,128)(2,1)}, u32[]{:S(2)}, u32[]{:S(2)}) collective-permute-start(bf16[2,704,256]{2,1,0:T(8,128)(2,1)} %collective-permute-done.11.refs_12_), channel_id=1, source_target_pairs={{0,8},{4,12},{8,24},{12,28},{24,16},{28,20},{16,0},{20,4},{1,9},{5... | collective-permute-start | bytes 2162696 | tf_op jit(solution)/shard_map/ppermute | solution.py:57
  168.0 17.0 %all-to-all-start.4 = ((bf16[4,64,2176]{2,1,0:T(8,128)(2,1)}), bf16[4,64,2176]{2,1,0:T(8,128)(2,1)S(1)}, u32[]{:S(2)}, u32[]{:S(2)}) async-start(bf16[4,64,2176]{2,1,0:T(8,128)(2,1)} %concatenate.34), calls=%async_computation.4 | async-start | bytes 2228224 | tf_op jit(solution)/shard_map/all_to_all | solution.py:27
  172.9 13.2 %copy-start.24 = (bf16[2,704,256]{2,1,0:T(8,128)(2,1)}, bf16[2,704,256]{2,1,0:T(8,128)(2,1)S(1)}, u32[]{:S(2)}) copy-start(bf16[2,704,256]{2,1,0:T(8,128)(2,1)S(1)} %collective-permute-done.8.refs_9_) | copy-start | bytes 2162692
  172.9 19.7 %collective-permute-start.3 = (bf16[2,256,1408]{2,1,0:T(8,128)(2,1)}, bf16[2,256,1408]{2,1,0:T(8,128)(2,1)}, u32[]{:S(2)}, u32[]{:S(2)}) collective-permute-start(bf16[2,256,1408]{2,1,0:T(8,128)(2,1)} %collective-permute-done.2.refs_2_), channel_id=1, source_target_pairs={{0,4},{4,0},{8,12},{12,8},{16,20},{20,16},{24,28},{28,24},{1,5},{5... | collective-permute-start | bytes 4325384 | tf_op jit(solution)/shard_map/ppermute | solution.py:58
  173.0 30.2 %collective-permute-start.5 = (bf16[2,256,1408]{2,1,0:T(8,128)(2,1)}, bf16[2,256,1408]{2,1,0:T(8,128)(2,1)}, u32[]{:S(2)}, u32[]{:S(2)}) collective-permute-start(bf16[2,256,1408]{2,1,0:T(8,128)(2,1)} %collective-permute-done.4.refs_4_), channel_id=1, source_target_pairs={{0,4},{4,0},{8,12},{12,8},{16,20},{20,16},{24,28},{28,24},{1,5},{5... | collective-permute-start | bytes 4325384 | tf_op jit(solution)/shard_map/ppermute | solution.py:58
  173.5 29.7 %collective-permute-start.7 = (bf16[2,256,1408]{2,1,0:T(8,128)(2,1)}, bf16[2,256,1408]{2,1,0:T(8,128)(2,1)}, u32[]{:S(2)}, u32[]{:S(2)}) collective-permute-start(bf16[2,256,1408]{2,1,0:T(8,128)(2,1)} %collective-permute-done.6.refs_6_), channel_id=1, source_target_pairs={{0,4},{4,0},{8,12},{12,8},{16,20},{20,16},{24,28},{28,24},{1,5},{5... | collective-permute-start | bytes 4325384 | tf_op jit(solution)/shard_map/ppermute | solution.py:58
  173.8 18.8 %collective-permute-start.12 = (bf16[2,704,256]{2,1,0:T(8,128)(2,1)}, bf16[2,704,256]{2,1,0:T(8,128)(2,1)}, u32[]{:S(2)}, u32[]{:S(2)}) collective-permute-start(bf16[2,704,256]{2,1,0:T(8,128)(2,1)} %collective-permute-done.11.refs_12_), channel_id=1, source_target_pairs={{0,4},{4,0},{8,12},{12,8},{16,20},{20,16},{24,28},{28,24},{1,5},{5... | collective-permute-start | bytes 2162696 | tf_op jit(solution)/shard_map/ppermute | solution.py:58
  183.9 8.7 %collective-permute-start.14 = (bf16[2,704,256]{2,1,0:T(8,128)(2,1)}, bf16[2,704,256]{2,1,0:T(8,128)(2,1)}, u32[]{:S(2)}, u32[]{:S(2)}) collective-permute-start(bf16[2,704,256]{2,1,0:T(8,128)(2,1)} %collective-permute-done.13.refs_14_), channel_id=1, source_target_pairs={{0,4},{4,0},{8,12},{12,8},{16,20},{20,16},{24,28},{28,24},{1,5},{5... | collective-permute-start | bytes 2162696 | tf_op jit(solution)/shard_map/ppermute | solution.py:58
  186.1 17.1 %all-to-all-start.3 = ((bf16[4,64,2048]{2,1,0:T(8,128)(2,1)}), bf16[4,64,2048]{2,1,0:T(8,128)(2,1)S(1)}, u32[]{:S(2)}, u32[]{:S(2)}) async-start(bf16[4,64,2048]{2,1,0:T(8,128)(2,1)} %broadcast_in_dim.157), calls=%async_computation.3 | async-start | bytes 2097152 | tf_op jit(solution)/shard_map/all_to_all | solution.py:27
  222.9 16.7 %all-to-all-start.6 = ((bf16[4,64,2048]{2,1,0:T(8,128)(2,1)}), bf16[4,64,2048]{2,1,0:T(8,128)(2,1)S(1)}, u32[]{:S(2)}, u32[]{:S(2)}) async-start(bf16[4,64,2048]{2,1,0:T(8,128)(2,1)} %bitcast.84), calls=%async_computation.6 | async-start | bytes 2097152 | tf_op jit(solution)/shard_map/all_to_all | solution.py:27
  239.6 17.3 %all-to-all-start.5 = ((bf16[4,64,2176]{2,1,0:T(8,128)(2,1)}), bf16[4,64,2176]{2,1,0:T(8,128)(2,1)S(1)}, u32[]{:S(2)}, u32[]{:S(2)}) async-start(bf16[4,64,2176]{2,1,0:T(8,128)(2,1)} %bitcast.34), calls=%async_computation.5 | async-start | bytes 2228224 | tf_op jit(solution)/shard_map/all_to_all | solution.py:27
  (16 other events, 41.7 us)
